TPU v7x, 256 devices: a whole 4x4x8 slice. The times are simulated.
256 devices in a mesh: quad: 8 (over z_lo, core), dom: 32 (over x, y, z_hi).
Axes of the slice: x: 4, y: 4, z: 8 (z_hi: 2, z_lo: 4; z = z_hi * 4 + z_lo), core: 2. Of those that a mesh axis runs over, the one named last changes fastest.
Arguments:
- probes: float32 [2, 64, 256, 128], P(None, None, 'dom'), may hold values from -6 to 6
- mass_weights: float32 [256, 128], P('dom'), may hold values from 0.8 to 1.25
- blocks: float32 [2, 256, 128, 128], P(None, 'dom'), may hold values from -4 to 4
- couplings: float32 [2, 6, 256, 128], P(None, None, 'dom'), may hold values from -0.25 to 0.25
Outputs:
- moments: float32 [64, 4, 2, 256, 128], P('quad', None, None, 'dom')
- projected: float32 [2, 8, 64, 64], replicated
All inputs are finite; a program needn't handle non-finite values.
Results may differ from a plain program's by a relative error of at most 0.0001.
Values sent between devices are 32-bit elements; how exact they have to be, the bound alone decides.
A program may use at most 64 MiB of HBM per device.

v0:
```python
import math
import jax
import jax.numpy as jnp
from jax import lax
from jax.sharding import PartitionSpec as P

NQ = 16
ITERS = 4
MOM = 4
PRECISE = lax.Precision.HIGHEST
RADIUS = 2.0
OFFSETS = (-3, -2, -1, 1, 2, 3)


def with_halo(cells, sides, width):
    for axis, dim in sides:
        count = lax.axis_size(axis)
        ends = count - 1
        head = lax.slice_in_dim(cells, 0, width, axis=dim)
        tail = lax.slice_in_dim(cells, cells.shape[dim] - width, cells.shape[dim], axis=dim)
        cells = jnp.concatenate(
            [
                lax.ppermute(tail, axis, [(i, (i + 1) % count) for i in range(ends)]),
                cells,
                lax.ppermute(head, axis, [((i + 1) % count, i) for i in range(ends)]),
            ],
            axis=dim,
        )
    return cells


def shift_angles(shift_index, total_shifts):
    return 2.0 * math.pi / total_shifts * (shift_index.astype(jnp.float32) + 0.5)


def moment_weights(angles, moment_count, scale):
    orders = jnp.arange(1, moment_count + 1, dtype=jnp.float32)
    phases = orders[:, None] * angles[None, :]
    return (scale * jnp.cos(phases), scale * jnp.sin(phases))


def sweep(field, padded, blocks, couplings, zmass_re, zmass_im, inverse_re, inverse_im, source):
    rim_depth = max(OFFSETS)
    line_count = field.shape[3]
    field_re = field[0]
    field_im = field[1]
    image_re = jnp.einsum("spxj,xij->spxi", field_re, blocks[0], precision=PRECISE) - jnp.einsum(
        "spxj,xij->spxi", field_im, blocks[1], precision=PRECISE
    )
    image_im = jnp.einsum("spxj,xij->spxi", field_im, blocks[0], precision=PRECISE) + jnp.einsum(
        "spxj,xij->spxi", field_re, blocks[1], precision=PRECISE
    )
    for position, offset in enumerate(OFFSETS):
        neighbour = padded[:, :, :, rim_depth + offset : rim_depth + offset + line_count]
        coup_re = couplings[0, position]
        coup_im = couplings[1, position]
        image_re = image_re + coup_re * neighbour[0] - coup_im * neighbour[1]
        image_im = image_im + coup_re * neighbour[1] + coup_im * neighbour[0]
    resid_re = source[0] - (zmass_re * field_re - zmass_im * field_im) + image_re
    resid_im = source[1] - (zmass_re * field_im + zmass_im * field_re) + image_im
    return jnp.stack(
        [
            field_re + resid_re * inverse_re - resid_im * inverse_im,
            field_im + resid_re * inverse_im + resid_im * inverse_re,
        ]
    )


def moment_block(field_part, weight_re, weight_im):
    sum_re = jnp.einsum("ks,spxi->pkxi", weight_re, field_part[0], precision=PRECISE) - jnp.einsum(
        "ks,spxi->pkxi", weight_im, field_part[1], precision=PRECISE
    )
    sum_im = jnp.einsum("ks,spxi->pkxi", weight_re, field_part[1], precision=PRECISE) + jnp.einsum(
        "ks,spxi->pkxi", weight_im, field_part[0], precision=PRECISE
    )
    return jnp.stack([sum_re, sum_im], axis=2)


def project(gram_re, gram_im, angles, scale):
    proj_re, proj_im = moment_weights(angles, 2 * MOM, scale)
    mixed_re = jnp.einsum("ks,spq->kpq", proj_re, gram_re, precision=PRECISE) - jnp.einsum(
        "ks,spq->kpq", proj_im, gram_im, precision=PRECISE
    )
    mixed_im = jnp.einsum("ks,spq->kpq", proj_re, gram_im, precision=PRECISE) + jnp.einsum(
        "ks,spq->kpq", proj_im, gram_re, precision=PRECISE
    )
    return jnp.stack([mixed_re, mixed_im])


def on_device(probes, mass_weights, blocks, couplings):
    rim_depth = max(OFFSETS)
    shift_count = NQ // lax.axis_size("quad")
    probe_count = probes.shape[1]
    owned_probes = probe_count // lax.axis_size("quad")
    line_count = probes.shape[2]
    row_width = probes.shape[3]
    total_lines = line_count * lax.axis_size("dom")
    shift_index = lax.axis_index("quad") * shift_count + jnp.arange(shift_count, dtype=jnp.int32)
    angles = shift_angles(shift_index, NQ)
    zmass_re = (RADIUS * jnp.cos(angles))[:, None, None, None] * mass_weights[None, None]
    zmass_im = (RADIUS * jnp.sin(angles))[:, None, None, None] * mass_weights[None, None]
    diagonal = jnp.diagonal(blocks, axis1=2, axis2=3)
    denom_re = zmass_re - diagonal[0]
    denom_im = zmass_im - diagonal[1]
    modulus = denom_re * denom_re + denom_im * denom_im
    inverse_re = denom_re / modulus
    inverse_im = -denom_im / modulus
    source = mass_weights[None, None] * probes
    field = jnp.stack(
        [
            source[0] * inverse_re - source[1] * inverse_im,
            source[0] * inverse_im + source[1] * inverse_re,
        ]
    )
    for step in range(ITERS - 1):
        padded = with_halo(field, (("dom", 3),), rim_depth)
        field = sweep(
            field, padded, blocks, couplings, zmass_re, zmass_im, inverse_re, inverse_im, source
        )
    weight_re, weight_im = moment_weights(angles, MOM, RADIUS / NQ)
    field_rows = lax.slice_in_dim(field, 0, owned_probes * lax.axis_size("quad"), axis=2)
    moments = lax.psum_scatter(
        moment_block(field_rows, weight_re, weight_im), "quad", scatter_dimension=0, tiled=True
    )
    gram_re = jnp.einsum("pxi,sqxi->spq", probes[0], field[0], precision=PRECISE) + jnp.einsum(
        "pxi,sqxi->spq", probes[1], field[1], precision=PRECISE
    )
    gram_im = jnp.einsum("pxi,sqxi->spq", probes[0], field[1], precision=PRECISE) - jnp.einsum(
        "pxi,sqxi->spq", probes[1], field[0], precision=PRECISE
    )
    scale = RADIUS / (NQ * total_lines * row_width)
    projected = lax.psum(project(gram_re, gram_im, angles, scale), ("quad", "dom"))
    return (moments, projected)


def solution(mesh):
    return jax.shard_map(
        on_device,
        mesh=mesh,
        in_specs=(
            P(None, None, "dom", None),
            P("dom", None),
            P(None, "dom", None, None),
            P(None, None, "dom", None),
        ),
        out_specs=(P("quad", None, None, "dom", None), P()),
        check_vma=False,
    )
```

profile of v0, /device:TPU:2, one launch (start us, length us, event | category | flops | bytes accessed | tf_op | source)
XLA Modules:
  0.0 444.9 jit_solution(10704677841827037540)
XLA Ops:
  8.1 13.3 %copy.50 = f32[2,8,128,128]{1,0,3,2:T(2,128)} copy(f32[2,8,128,128]{3,2,1,0:T(8,128)} %param.6) | data formatting | bytes 2097152 | tf_op args[2]
  21.3 6.7 %gather_fusion = f32[128,2,8]{2,1,0:T(2,128)S(1)} fusion(f32[2,8,128,128]{1,0,3,2:T(2,128)} %copy.50, s32[128]{0:T(128)S(1)} %or_bitcast_fusion), kind=kCustom, calls=%fused_computation | custom fusion | bytes 17408 | tf_op jit(solution)/shard_map/jit(diagonal)/gather | solution.py:102
  28.0 0.1 fusion.130
  28.7 0.2 multiply_subtract_fusion.3
  28.9 11.7 %collective-permute-start.1 = (f32[2,2,64,3,128]{4,2,1,3,0:T(8,128)S(1)}, f32[2,2,64,3,128]{4,2,1,3,0:T(8,128)S(1)}, u32[]{:S(2)}, u32[]{:S(2)}) collective-permute-start(f32[2,2,64,3,128]{4,2,1,3,0:T(8,128)S(1)} %get-tuple-element.24), channel_id=1, source_target_pairs={{1,0},{2,1},{3,2},{4,3},{5,4},{6,5},{7,6},{8,7},{9,8},{10,9},{11,1... | collective-permute-start | bytes 1179656 | tf_op jit(solution)/shard_map/ppermute | solution.py:25
  40.6 1.9 collective-permute-start
  42.5 1.2 fusion.30
  43.9 1.2 fusion.28
  45.1 7.2 %collective-permute-done.1 = f32[2,2,64,3,128]{4,2,1,3,0:T(8,128)S(1)} collective-permute-done((f32[2,2,64,3,128]{4,2,1,3,0:T(8,128)S(1)}, f32[2,2,64,3,128]{4,2,1,3,0:T(8,128)S(1)}, u32[]{:S(2)}, u32[]{:S(2)}) %collective-permute-start.1) | collective-permute-done | bytes 393248 | tf_op jit(solution)/shard_map/ppermute | solution.py:25
  52.3 21.3 %collective-permute-done = f32[2,2,64,3,128]{4,2,1,3,0:T(8,128)S(1)} collective-permute-done((f32[2,2,64,3,128]{4,2,1,3,0:T(8,128)S(1)}, f32[2,2,64,3,128]{4,2,1,3,0:T(8,128)S(1)}, u32[]{:S(2)}, u32[]{:S(2)}) %collective-permute-start) | collective-permute-done | bytes 393248 | tf_op jit(solution)/shard_map/ppermute | solution.py:23
  73.6 0.4 pad_maximum_fusion.1
  74.0 1.9 subtract_add_fusion.2
  75.9 2.2 multiply_add_fusion.2
  78.2 8.9 %collective-permute-start.3 = (f32[2,2,64,3,128]{4,2,1,3,0:T(8,128)S(1)}, f32[2,2,64,3,128]{4,2,1,3,0:T(8,128)S(1)}, u32[]{:S(2)}, u32[]{:S(2)}) collective-permute-start(f32[2,2,64,3,128]{4,2,1,3,0:T(8,128)S(1)} %get-tuple-element.20), channel_id=1, source_target_pairs={{1,0},{2,1},{3,2},{4,3},{5,4},{6,5},{7,6},{8,7},{9,8},{10,9},{11,1... | collective-permute-start | bytes 1179656 | tf_op jit(solution)/shard_map/ppermute | solution.py:25
  87.1 1.9 collective-permute-start.2
  89.0 1.2 fusion.26
  90.3 1.2 fusion.24
  91.5 12.3 %collective-permute-done.3 = f32[2,2,64,3,128]{4,2,1,3,0:T(8,128)S(1)} collective-permute-done((f32[2,2,64,3,128]{4,2,1,3,0:T(8,128)S(1)}, f32[2,2,64,3,128]{4,2,1,3,0:T(8,128)S(1)}, u32[]{:S(2)}, u32[]{:S(2)}) %collective-permute-start.3) | collective-permute-done | bytes 393248 | tf_op jit(solution)/shard_map/ppermute | solution.py:25
  103.8 8.8 %collective-permute-done.2 = f32[2,2,64,3,128]{4,2,1,3,0:T(8,128)S(1)} collective-permute-done((f32[2,2,64,3,128]{4,2,1,3,0:T(8,128)S(1)}, f32[2,2,64,3,128]{4,2,1,3,0:T(8,128)S(1)}, u32[]{:S(2)}, u32[]{:S(2)}) %collective-permute-start.2) | collective-permute-done | bytes 393248 | tf_op jit(solution)/shard_map/ppermute | solution.py:23
  112.6 0.4 pad_maximum_fusion.2
  112.9 1.8 subtract_add_fusion.1
  114.8 2.1 multiply_add_fusion.1
  116.9 7.4 %collective-permute-start.5 = (f32[2,2,64,3,128]{4,2,1,3,0:T(8,128)S(1)}, f32[2,2,64,3,128]{4,2,1,3,0:T(8,128)S(1)}, u32[]{:S(2)}, u32[]{:S(2)}) collective-permute-start(f32[2,2,64,3,128]{4,2,1,3,0:T(8,128)S(1)} %get-tuple-element.16), channel_id=1, source_target_pairs={{1,0},{2,1},{3,2},{4,3},{5,4},{6,5},{7,6},{8,7},{9,8},{10,9},{11,1... | collective-permute-start | bytes 1179656 | tf_op jit(solution)/shard_map/ppermute | solution.py:25
  124.3 3.7 collective-permute-start.4
  128.1 1.2 fusion.22
  129.3 1.2 fusion.20
  130.5 1.3 collective-permute-done.5
  131.8 22.8 %collective-permute-done.4 = f32[2,2,64,3,128]{4,2,1,3,0:T(8,128)S(1)} collective-permute-done((f32[2,2,64,3,128]{4,2,1,3,0:T(8,128)S(1)}, f32[2,2,64,3,128]{4,2,1,3,0:T(8,128)S(1)}, u32[]{:S(2)}, u32[]{:S(2)}) %collective-permute-start.4) | collective-permute-done | bytes 393248 | tf_op jit(solution)/shard_map/ppermute | solution.py:23
  154.6 0.3 pad_maximum_fusion.3
  154.8 1.9 subtract_add_fusion
  156.8 2.1 multiply_subtract_fusion
  158.8 2.2 fusion.36
  161.0 2.2 fusion.40
  163.2 0.6 convolution_bitcast_fusion
  163.8 0.6 convolution_bitcast_fusion.2
  164.4 2.5 fusion
  166.9 2.3 fusion.1
  169.2 0.6 fusion.13
  169.9 0.6 fusion.11
  170.6 0.5 fusion.89
  171.1 0.5 fusion.91
  171.7 0.5 fusion.9
  172.2 0.5 fusion.8
  172.7 0.8 pad_maximum_fusion.4
  173.7 0.5 pad_maximum_fusion
  174.2 1.5 copy.60
  175.8 259.7 %all-reduce.2.cloned.1.call-done = f32[2,8,64,64]{3,1,2,0:T(8,128)} async-done(((f32[2,8,64,64]{3,1,2,0:T(8,128)}), f32[2,8,64,64]{3,1,2,0:T(8,128)}) %all-reduce.2.cloned.1.call-update) | async-done | bytes 262160 | tf_op jit(solution)/shard_map/psum | solution.py:132
  435.5 1.9 copy.67
  (32 shorter events, 1.1 us)
Async XLA Ops:
  8.0 427.5 %all-reduce.2.cloned.1.call-start = ((), (), s32[]{:S(2)}) async-start(), calls=%async_computation.2 | async-start | bytes 1048576 | tf_op jit(solution)/shard_map/psum | solution.py:132
  8.1 20.3 %copy-start.1 = (f32[2,64,8,128]{3,2,1,0:T(8,128)S(1)}, f32[2,64,8,128]{3,2,1,0:T(8,128)}, u32[]{:S(2)}) copy-start(f32[2,64,8,128]{3,2,1,0:T(8,128)} %param.4) | copy-start | bytes 1572868
  8.1 20.3 %copy-start.3 = (f32[8,128]{1,0:T(8,128)S(1)}, f32[8,128]{1,0:T(8,128)}, u32[]{:S(2)}) copy-start(f32[8,128]{1,0:T(8,128)} %param.5) | copy-start | bytes 12292
  28.7 13.9 %copy-start = (f32[2,8,128,128]{3,2,1,0:T(8,128)S(1)}, f32[2,8,128,128]{3,2,1,0:T(8,128)}, u32[]{:S(2)}) copy-start(f32[2,8,128,128]{3,2,1,0:T(8,128)} %param.6) | copy-start | bytes 3145732
  28.9 14.9 %copy-start.2 = (f32[2,6,8,128]{3,2,1,0:T(8,128)S(1)}, f32[2,6,8,128]{3,2,1,0:T(8,128)}, u32[]{:S(2)}) copy-start(f32[2,6,8,128]{3,2,1,0:T(8,128)} %param.7) | copy-start | bytes 147460
  28.9 23.3 %collective-permute-start.1 = (f32[2,2,64,3,128]{4,2,1,3,0:T(8,128)S(1)}, f32[2,2,64,3,128]{4,2,1,3,0:T(8,128)S(1)}, u32[]{:S(2)}, u32[]{:S(2)}) collective-permute-start(f32[2,2,64,3,128]{4,2,1,3,0:T(8,128)S(1)} %get-tuple-element.24), channel_id=1, source_target_pairs={{1,0},{2,1},{3,2},{4,3},{5,4},{6,5},{7,6},{8,7},{9,8},{10,9},{11,1... | collective-permute-start | bytes 1179656 | tf_op jit(solution)/shard_map/ppermute | solution.py:25
  40.6 33.0 %collective-permute-start = (f32[2,2,64,3,128]{4,2,1,3,0:T(8,128)S(1)}, f32[2,2,64,3,128]{4,2,1,3,0:T(8,128)S(1)}, u32[]{:S(2)}, u32[]{:S(2)}) collective-permute-start(f32[2,2,64,3,128]{4,2,1,3,0:T(8,128)S(1)} %get-tuple-element.25), channel_id=1, source_target_pairs={{0,1},{1,2},{2,3},{3,4},{4,5},{5,6},{6,7},{7,8},{8,9},{9,10},{10,1... | collective-permute-start | bytes 1179656 | tf_op jit(solution)/shard_map/ppermute | solution.py:23
  78.2 25.6 %collective-permute-start.3 = (f32[2,2,64,3,128]{4,2,1,3,0:T(8,128)S(1)}, f32[2,2,64,3,128]{4,2,1,3,0:T(8,128)S(1)}, u32[]{:S(2)}, u32[]{:S(2)}) collective-permute-start(f32[2,2,64,3,128]{4,2,1,3,0:T(8,128)S(1)} %get-tuple-element.20), channel_id=1, source_target_pairs={{1,0},{2,1},{3,2},{4,3},{5,4},{6,5},{7,6},{8,7},{9,8},{10,9},{11,1... | collective-permute-start | bytes 1179656 | tf_op jit(solution)/shard_map/ppermute | solution.py:25
  87.1 25.5 %collective-permute-start.2 = (f32[2,2,64,3,128]{4,2,1,3,0:T(8,128)S(1)}, f32[2,2,64,3,128]{4,2,1,3,0:T(8,128)S(1)}, u32[]{:S(2)}, u32[]{:S(2)}) collective-permute-start(f32[2,2,64,3,128]{4,2,1,3,0:T(8,128)S(1)} %get-tuple-element.21), channel_id=1, source_target_pairs={{0,1},{1,2},{2,3},{3,4},{4,5},{5,6},{6,7},{7,8},{8,9},{9,10},{10,1... | collective-permute-start | bytes 1179656 | tf_op jit(solution)/shard_map/ppermute | solution.py:23
  116.9 14.9 %collective-permute-start.5 = (f32[2,2,64,3,128]{4,2,1,3,0:T(8,128)S(1)}, f32[2,2,64,3,128]{4,2,1,3,0:T(8,128)S(1)}, u32[]{:S(2)}, u32[]{:S(2)}) collective-permute-start(f32[2,2,64,3,128]{4,2,1,3,0:T(8,128)S(1)} %get-tuple-element.16), channel_id=1, source_target_pairs={{1,0},{2,1},{3,2},{4,3},{5,4},{6,5},{7,6},{8,7},{9,8},{10,9},{11,1... | collective-permute-start | bytes 1179656 | tf_op jit(solution)/shard_map/ppermute | solution.py:25
  124.3 30.2 %collective-permute-start.4 = (f32[2,2,64,3,128]{4,2,1,3,0:T(8,128)S(1)}, f32[2,2,64,3,128]{4,2,1,3,0:T(8,128)S(1)}, u32[]{:S(2)}, u32[]{:S(2)}) collective-permute-start(f32[2,2,64,3,128]{4,2,1,3,0:T(8,128)S(1)} %get-tuple-element.17), channel_id=1, source_target_pairs={{0,1},{1,2},{2,3},{3,4},{4,5},{5,6},{6,7},{7,8},{8,9},{9,10},{10,1... | collective-permute-start | bytes 1179656 | tf_op jit(solution)/shard_map/ppermute | solution.py:23
  173.6 263.8 %reduce-scatter.2.cloned.1.call-start = ((), (), s32[]{:S(2)}) async-start(), calls=%async_computation.1 | async-start | bytes 2359296 | tf_op jit(solution)/shard_map/reduce_scatter | solution.py:122
Sparse Core Ops, SparseCore 0:
  173.7 261.7 all-reduce.1
Sparse Core Ops, SparseCore 1:
  177.2 49.0 reduce-scatter.1
where the time goes:
time: 446 us; the launch traced here: 445 us
  waiting for transfers between devices  333 us (75%)
  starting transfers between devices  35.6 us (8%)
  matrix products  32.9 us (7%)
  local copies, waits for them, and re-layouts  24 us (5%)
  between operations  15.9 us (4%)
    psum x1, waiting for transfers between devices, on_device(): lax.psum(project(gram_re, gram_im, angles, scale), ('quad', 'dom'))  260 us
    ppermute x3, waiting for transfers between devices, with_halo(): lax.ppermute(tail, axis, [(i, (i + 1) % count) for i in range(ends)])  52.9 us
    ppermute x3, starting transfers between devices, with_halo(): lax.ppermute(head, axis, [((i + 1) % count, i) for i in range(ends)])  28 us
    ppermute x3, waiting for transfers between devices, with_halo(): lax.ppermute(head, axis, [((i + 1) % count, i) for i in range(ends)])  20.8 us
    unnamed x10, local copies, waits for them, and re-layouts  15.2 us
  transfers between devices with their start and end apart: 8, of which 7 were waited for; matrix products, arithmetic and copies ran while one was open for 3% of the time, Pallas kernels for 0%

commit v1 on v0

--- a/solution.py
+++ b/solution.py
@@ -10,6 +10,10 @@
 PRECISE = lax.Precision.HIGHEST
 RADIUS = 2.0
 OFFSETS = (-3, -2, -1, 1, 2, 3)
+
+
+def place_cubes(shard_in):
+    return lax.psum(lax.psum(shard_in, "quad"), "dom")
 
 
 def with_halo(cells, sides, width):
@@ -129,7 +133,7 @@
         "pxi,sqxi->spq", probes[1], field[0], precision=PRECISE
     )
     scale = RADIUS / (NQ * total_lines * row_width)
-    projected = lax.psum(project(gram_re, gram_im, angles, scale), ("quad", "dom"))
+    projected = place_cubes(project(gram_re, gram_im, angles, scale))
     return (moments, projected)
 
 

time: 446 us -> 728 us (1.63)
  waiting for transfers between devices: 333 us -> 617 us
    psum x1 -> x2, waiting for transfers between devices: 260 us -> 497 us  [place_cubes(): return lax.psum(lax.psum(shard_in, 'quad'), 'dom')]
    reduce_scatter x1, waiting for transfers between devices: 0.01 us -> 46.7 us  [on_device(): lax.psum_scatter(moment_block(field_rows, weight_re, weight_im), 'quad',...]
  transfers between devices with their start and end apart: 8 -> 9, of which waited for: 7 -> 9; matrix products, arithmetic and copies ran while one was open for 3% -> 2% of each run, Pallas kernels for 0% -> 0%
where the time goes in v1:
time: 728 us; the launch traced here: 727 us
  waiting for transfers between devices  617 us (85%)
  starting transfers between devices  35.8 us (5%)
  matrix products  32.7 us (4%)
  local copies, waits for them, and re-layouts  24 us (3%)
  between operations  14.2 us (2%)
    psum x2, waiting for transfers between devices, place_cubes(): return lax.psum(lax.psum(shard_in, 'quad'), 'dom')  497 us
    ppermute x3, waiting for transfers between devices, with_halo(): lax.ppermute(tail, axis, [(i, (i + 1) % count) for i in range(ends)])  52.1 us
    reduce_scatter x1, waiting for transfers between devices, on_device(): lax.psum_scatter(moment_block(field_rows, weight_re, weight_im), 'quad',...  46.7 us
    ppermute x3, starting transfers between devices, with_halo(): lax.ppermute(head, axis, [((i + 1) % count, i) for i in range(ends)])  28 us
    ppermute x3, waiting for transfers between devices, with_halo(): lax.ppermute(head, axis, [((i + 1) % count, i) for i in range(ends)])  21.4 us
    unnamed x10, local copies, waits for them, and re-layouts  15.2 us
  transfers between devices with their start and end apart: 9, of which 9 were waited for; matrix products, arithmetic and copies ran while one was open for 2% of the time, Pallas kernels for 0%

profile of v1, /device:TPU:2, one launch (start us, length us, event | category | flops | bytes accessed | tf_op | source)
XLA Modules:
  0.0 726.6 jit_solution(16513765652101253332)
XLA Ops:
  7.2 13.3 %copy.50 = f32[2,8,128,128]{1,0,3,2:T(2,128)} copy(f32[2,8,128,128]{3,2,1,0:T(8,128)} %param.6) | data formatting | bytes 2097152 | tf_op args[2]
  20.5 6.7 gather_fusion
  28.1 11.7 %collective-permute-start.1 = (f32[2,2,64,3,128]{4,2,1,3,0:T(8,128)S(1)}, f32[2,2,64,3,128]{4,2,1,3,0:T(8,128)S(1)}, u32[]{:S(2)}, u32[]{:S(2)}) collective-permute-start(f32[2,2,64,3,128]{4,2,1,3,0:T(8,128)S(1)} %get-tuple-element.24), channel_id=1, source_target_pairs={{1,0},{2,1},{3,2},{4,3},{5,4},{6,5},{7,6},{8,7},{9,8},{10,9},{11,1... | collective-permute-start | bytes 1179656 | tf_op jit(solution)/shard_map/ppermute | solution.py:29
  39.7 1.9 collective-permute-start
  41.7 1.2 fusion.30
  43.0 1.2 fusion.28
  44.2 7.2 collective-permute-done.1
  51.4 21.3 %collective-permute-done = f32[2,2,64,3,128]{4,2,1,3,0:T(8,128)S(1)} collective-permute-done((f32[2,2,64,3,128]{4,2,1,3,0:T(8,128)S(1)}, f32[2,2,64,3,128]{4,2,1,3,0:T(8,128)S(1)}, u32[]{:S(2)}, u32[]{:S(2)}) %collective-permute-start) | collective-permute-done | bytes 393248 | tf_op jit(solution)/shard_map/ppermute | solution.py:27
  72.7 0.4 pad_maximum_fusion.1
  73.1 1.9 subtract_add_fusion.2
  75.0 2.2 multiply_add_fusion.2
  77.3 8.9 %collective-permute-start.3 = (f32[2,2,64,3,128]{4,2,1,3,0:T(8,128)S(1)}, f32[2,2,64,3,128]{4,2,1,3,0:T(8,128)S(1)}, u32[]{:S(2)}, u32[]{:S(2)}) collective-permute-start(f32[2,2,64,3,128]{4,2,1,3,0:T(8,128)S(1)} %get-tuple-element.20), channel_id=1, source_target_pairs={{1,0},{2,1},{3,2},{4,3},{5,4},{6,5},{7,6},{8,7},{9,8},{10,9},{11,1... | collective-permute-start | bytes 1179656 | tf_op jit(solution)/shard_map/ppermute | solution.py:29
  86.2 1.9 collective-permute-start.2
  88.2 1.2 fusion.26
  89.4 1.2 fusion.24
  90.6 12.9 %collective-permute-done.3 = f32[2,2,64,3,128]{4,2,1,3,0:T(8,128)S(1)} collective-permute-done((f32[2,2,64,3,128]{4,2,1,3,0:T(8,128)S(1)}, f32[2,2,64,3,128]{4,2,1,3,0:T(8,128)S(1)}, u32[]{:S(2)}, u32[]{:S(2)}) %collective-permute-start.3) | collective-permute-done | bytes 393248 | tf_op jit(solution)/shard_map/ppermute | solution.py:29
  103.5 8.1 %collective-permute-done.2 = f32[2,2,64,3,128]{4,2,1,3,0:T(8,128)S(1)} collective-permute-done((f32[2,2,64,3,128]{4,2,1,3,0:T(8,128)S(1)}, f32[2,2,64,3,128]{4,2,1,3,0:T(8,128)S(1)}, u32[]{:S(2)}, u32[]{:S(2)}) %collective-permute-start.2) | collective-permute-done | bytes 393248 | tf_op jit(solution)/shard_map/ppermute | solution.py:27
  111.6 0.4 pad_maximum_fusion.2
  112.0 1.8 subtract_add_fusion.1
  113.8 2.0 multiply_add_fusion.1
  115.9 7.5 %collective-permute-start.5 = (f32[2,2,64,3,128]{4,2,1,3,0:T(8,128)S(1)}, f32[2,2,64,3,128]{4,2,1,3,0:T(8,128)S(1)}, u32[]{:S(2)}, u32[]{:S(2)}) collective-permute-start(f32[2,2,64,3,128]{4,2,1,3,0:T(8,128)S(1)} %get-tuple-element.16), channel_id=1, source_target_pairs={{1,0},{2,1},{3,2},{4,3},{5,4},{6,5},{7,6},{8,7},{9,8},{10,9},{11,1... | collective-permute-start | bytes 1179656 | tf_op jit(solution)/shard_map/ppermute | solution.py:29
  123.3 3.8 collective-permute-start.4
  127.1 1.2 fusion.22
  128.3 1.2 fusion.20
  129.6 1.3 collective-permute-done.5
  130.9 22.7 %collective-permute-done.4 = f32[2,2,64,3,128]{4,2,1,3,0:T(8,128)S(1)} collective-permute-done((f32[2,2,64,3,128]{4,2,1,3,0:T(8,128)S(1)}, f32[2,2,64,3,128]{4,2,1,3,0:T(8,128)S(1)}, u32[]{:S(2)}, u32[]{:S(2)}) %collective-permute-start.4) | collective-permute-done | bytes 393248 | tf_op jit(solution)/shard_map/ppermute | solution.py:27
  153.6 0.4 pad_maximum_fusion.3
  153.9 1.8 subtract_add_fusion
  155.7 2.0 multiply_subtract_fusion
  157.8 0.6 convolution_bitcast_fusion
  158.3 0.6 convolution_bitcast_fusion.2
  158.9 2.2 fusion.36
  161.1 2.4 fusion
  163.5 0.6 fusion.13
  164.1 0.6 fusion.11
  164.8 0.5 fusion.89
  165.4 0.5 fusion.91
  165.9 0.8 fusion.9
  166.7 0.5 fusion.8
  167.2 0.8 pad_maximum_fusion.4
  168.2 2.2 fusion.40
  170.4 77.8 %all-reduce.3.cloned.1.call-done = f32[2,8,64,64]{3,1,2,0:T(8,128)} async-done(((f32[2,8,64,64]{3,1,2,0:T(8,128)}), f32[2,8,64,64]{3,1,2,0:T(8,128)}) %all-reduce.3.cloned.1.call-update) | async-done | bytes 262160 | tf_op jit(solution)/shard_map/psum | solution.py:16
  248.2 2.2 fusion.1
  250.5 0.5 pad_maximum_fusion
  251.0 1.5 copy.60
  252.6 418.9 %all-reduce.5.cloned.1.call-done = f32[2,8,64,64]{3,1,2,0:T(8,128)} async-done(((f32[2,8,64,64]{3,1,2,0:T(8,128)}), f32[2,8,64,64]{3,1,2,0:T(8,128)}) %all-reduce.5.cloned.1.call-update) | async-done | bytes 262160 | tf_op jit(solution)/shard_map/psum | solution.py:16
  671.4 1.9 copy.67
  673.4 46.7 %reduce-scatter.2.cloned.1.call-done = f32[8,4,2,8,128]{4,3,2,1,0:T(8,128)} async-done(((f32[64,4,2,8,128]{4,3,2,1,0:T(8,128)}), f32[8,4,2,8,128]{4,3,2,1,0:T(8,128)}) %reduce-scatter.2.cloned.1.call-update) | async-done | bytes 262160 | tf_op jit(solution)/shard_map/reduce_scatter | solution.py:126
  (35 shorter events, 1.3 us)
Async XLA Ops:
  7.2 241.0 %all-reduce.3.cloned.1.call-start = ((), (), s32[]{:S(2)}) async-start(), calls=%async_computation.2 | async-start | bytes 1048576 | tf_op jit(solution)/shard_map/psum | solution.py:16
  7.2 20.3 %copy-start.1 = (f32[2,64,8,128]{3,2,1,0:T(8,128)S(1)}, f32[2,64,8,128]{3,2,1,0:T(8,128)}, u32[]{:S(2)}) copy-start(f32[2,64,8,128]{3,2,1,0:T(8,128)} %param.4) | copy-start | bytes 1572868
  7.2 20.3 %copy-start.3 = (f32[8,128]{1,0:T(8,128)S(1)}, f32[8,128]{1,0:T(8,128)}, u32[]{:S(2)}) copy-start(f32[8,128]{1,0:T(8,128)} %param.5) | copy-start | bytes 12292
  27.8 13.8 %copy-start = (f32[2,8,128,128]{3,2,1,0:T(8,128)S(1)}, f32[2,8,128,128]{3,2,1,0:T(8,128)}, u32[]{:S(2)}) copy-start(f32[2,8,128,128]{3,2,1,0:T(8,128)} %param.6) | copy-start | bytes 3145732
  28.1 14.9 %copy-start.2 = (f32[2,6,8,128]{3,2,1,0:T(8,128)S(1)}, f32[2,6,8,128]{3,2,1,0:T(8,128)}, u32[]{:S(2)}) copy-start(f32[2,6,8,128]{3,2,1,0:T(8,128)} %param.7) | copy-start | bytes 147460
  28.1 23.3 %collective-permute-start.1 = (f32[2,2,64,3,128]{4,2,1,3,0:T(8,128)S(1)}, f32[2,2,64,3,128]{4,2,1,3,0:T(8,128)S(1)}, u32[]{:S(2)}, u32[]{:S(2)}) collective-permute-start(f32[2,2,64,3,128]{4,2,1,3,0:T(8,128)S(1)} %get-tuple-element.24), channel_id=1, source_target_pairs={{1,0},{2,1},{3,2},{4,3},{5,4},{6,5},{7,6},{8,7},{9,8},{10,9},{11,1... | collective-permute-start | bytes 1179656 | tf_op jit(solution)/shard_map/ppermute | solution.py:29
  39.7 33.0 %collective-permute-start = (f32[2,2,64,3,128]{4,2,1,3,0:T(8,128)S(1)}, f32[2,2,64,3,128]{4,2,1,3,0:T(8,128)S(1)}, u32[]{:S(2)}, u32[]{:S(2)}) collective-permute-start(f32[2,2,64,3,128]{4,2,1,3,0:T(8,128)S(1)} %get-tuple-element.25), channel_id=1, source_target_pairs={{0,1},{1,2},{2,3},{3,4},{4,5},{5,6},{6,7},{7,8},{8,9},{9,10},{10,1... | collective-permute-start | bytes 1179656 | tf_op jit(solution)/shard_map/ppermute | solution.py:27
  77.3 26.2 %collective-permute-start.3 = (f32[2,2,64,3,128]{4,2,1,3,0:T(8,128)S(1)}, f32[2,2,64,3,128]{4,2,1,3,0:T(8,128)S(1)}, u32[]{:S(2)}, u32[]{:S(2)}) collective-permute-start(f32[2,2,64,3,128]{4,2,1,3,0:T(8,128)S(1)} %get-tuple-element.20), channel_id=1, source_target_pairs={{1,0},{2,1},{3,2},{4,3},{5,4},{6,5},{7,6},{8,7},{9,8},{10,9},{11,1... | collective-permute-start | bytes 1179656 | tf_op jit(solution)/shard_map/ppermute | solution.py:29
  86.2 25.4 %collective-permute-start.2 = (f32[2,2,64,3,128]{4,2,1,3,0:T(8,128)S(1)}, f32[2,2,64,3,128]{4,2,1,3,0:T(8,128)S(1)}, u32[]{:S(2)}, u32[]{:S(2)}) collective-permute-start(f32[2,2,64,3,128]{4,2,1,3,0:T(8,128)S(1)} %get-tuple-element.21), channel_id=1, source_target_pairs={{0,1},{1,2},{2,3},{3,4},{4,5},{5,6},{6,7},{7,8},{8,9},{9,10},{10,1... | collective-permute-start | bytes 1179656 | tf_op jit(solution)/shard_map/ppermute | solution.py:27
  115.9 15.0 %collective-permute-start.5 = (f32[2,2,64,3,128]{4,2,1,3,0:T(8,128)S(1)}, f32[2,2,64,3,128]{4,2,1,3,0:T(8,128)S(1)}, u32[]{:S(2)}, u32[]{:S(2)}) collective-permute-start(f32[2,2,64,3,128]{4,2,1,3,0:T(8,128)S(1)} %get-tuple-element.16), channel_id=1, source_target_pairs={{1,0},{2,1},{3,2},{4,3},{5,4},{6,5},{7,6},{8,7},{9,8},{10,9},{11,1... | collective-permute-start | bytes 1179656 | tf_op jit(solution)/shard_map/ppermute | solution.py:29
  123.3 30.2 %collective-permute-start.4 = (f32[2,2,64,3,128]{4,2,1,3,0:T(8,128)S(1)}, f32[2,2,64,3,128]{4,2,1,3,0:T(8,128)S(1)}, u32[]{:S(2)}, u32[]{:S(2)}) collective-permute-start(f32[2,2,64,3,128]{4,2,1,3,0:T(8,128)S(1)} %get-tuple-element.17), channel_id=1, source_target_pairs={{0,1},{1,2},{2,3},{3,4},{4,5},{5,6},{6,7},{7,8},{8,9},{9,10},{10,1... | collective-permute-start | bytes 1179656 | tf_op jit(solution)/shard_map/ppermute | solution.py:27
  168.1 503.3 %all-reduce.5.cloned.1.call-start = ((), (), s32[]{:S(2)}) async-start(), calls=%async_computation.3 | async-start | bytes 1048576 | tf_op jit(solution)/shard_map/psum | solution.py:16
  248.2 471.9 %reduce-scatter.2.cloned.1.call-start = ((), (), s32[]{:S(2)}) async-start(), calls=%async_computation.1 | async-start | bytes 2359296 | tf_op jit(solution)/shard_map/reduce_scatter | solution.py:126
Sparse Core Ops, SparseCore 0:
  168.2 79.8 all-reduce.2
  250.9 420.4 all-reduce.4
  674.5 45.4 reduce-scatter.1
